TPU v7x, 32 devices: a whole 2x2x4 slice. The times are simulated.
32 devices in a mesh: grp: 2 (over x), group: 16 (over z, y, core).
Axes of the slice: x: 2, y: 2, z: 4, core: 2. Of those that a mesh axis runs over, the one named last changes fastest.
Arguments:
- query_pre: bfloat16 [4096, 2240], P(('grp', 'group')), parts along dimension 0, may hold values from -6 to 6
- key_pre: bfloat16 [4096, 2240], P(('grp', 'group')), parts along dimension 0, may hold values from -6 to 6
- values: bfloat16 [4096, 2240], P(('grp', 'group')), parts along dimension 0, may hold values from -6 to 6
- out_grad: bfloat16 [4096, 2240], P(('grp', 'group')), parts along dimension 0, may hold values from -6 to 6
- block_frame: int32 [64], P(('grp', 'group')), parts along dimension 0, may hold values from 0 to 20
- frame_embed: bfloat16 [21, 2240], replicated, may hold values from -3 to 3
Outputs:
- attn_out: bfloat16 [4096, 2240], P(('grp', 'group')), parts along dimension 0
- query_grad: bfloat16 [4096, 2240], P(('grp', 'group')), parts along dimension 0
- key_grad: bfloat16 [4096, 2240], P(('grp', 'group')), parts along dimension 0
- value_grad: bfloat16 [4096, 2240], P(('grp', 'group')), parts along dimension 0
There are 2 independent parts, one for each index of `grp`. A program takes and returns all parts, laid end to end along the dimension named above; an argument that names none is the same for every part. Nothing has to cross between parts.
All inputs are finite; a program needn't handle non-finite values.
Results may differ from a plain program's by a relative error of at most 0.0058.
Values sent between devices are 32-bit elements; how exact they have to be, the bound alone decides.
A program may use at most 320 MiB of HBM per device.

v0:
```python
import jax
import jax.numpy as jnp
from jax import lax
from jax.sharding import PartitionSpec as P

HEADS = 20
HD = 112
CL = 64


score_scale = 4.0


def prefix(part, axis, combine, identity, reverse):
    count = lax.axis_size(axis)
    place = lax.axis_index(axis)
    ahead = count - 1 - place if reverse else place
    gathered = lax.all_gather(part, axis)
    state = jnp.zeros_like(part) + jnp.asarray(identity, part.dtype)

    def one(hop, state):
        source = count - 1 - hop if reverse else hop
        return combine(state, lax.dynamic_index_in_dim(gathered, source, 0, False))

    return lax.fori_loop(0, ahead, one, state)


def add_pair(earlier, later):
    return earlier + later


def local(query_pre, key_pre, values, out_grad, block_frame, frame_embed):
    token_count = query_pre.shape[0]
    feature_width = query_pre.shape[1]
    n_blocks = token_count // CL
    frame_ids = jnp.arange(frame_embed.shape[0], dtype=jnp.int32)
    onehot = (block_frame[:, None] == frame_ids[None, :]).astype(jnp.bfloat16)
    frame_shift = jnp.dot(onehot, frame_embed, preferred_element_type=jnp.float32)
    key_in = (
        key_pre.reshape(n_blocks, CL, feature_width).astype(jnp.float32) + frame_shift[:, None, :]
    )
    key_act = jnp.maximum(key_in, 0.0).astype(jnp.bfloat16).reshape(n_blocks, CL, HEADS, HD)
    query_act = jnp.maximum(query_pre, 0).reshape(n_blocks, CL, HEADS, HD)
    value_rows = values.reshape(n_blocks, CL, HEADS, HD)
    grad_rows = out_grad.reshape(n_blocks, CL, HEADS, HD)
    position = lax.axis_index("group") * n_blocks + jnp.arange(n_blocks, dtype=jnp.int32) + 1
    row_scale = score_scale / (HD * jnp.sqrt((position * CL).astype(jnp.float32)))
    kv_each = jnp.einsum("cthi,cthj->chij", key_act, value_rows, preferred_element_type=jnp.float32)
    grad_each = row_scale[:, None, None, None] * jnp.einsum(
        "cthi,cthj->chij", query_act, grad_rows, preferred_element_type=jnp.float32
    )
    kv_local = jnp.sum(kv_each, axis=0)
    grad_local = jnp.sum(grad_each, axis=0)
    zero_state = jnp.zeros_like(kv_local)
    kv_before = prefix(kv_local, "group", add_pair, zero_state, False)
    grad_after = prefix(grad_local, "group", add_pair, zero_state, True)

    def forward(carry_state, block):
        query_block, grad_block, state_term, factor = block
        carry_state = carry_state + state_term
        rounded = carry_state.astype(jnp.bfloat16)
        result = factor * jnp.einsum(
            "thi,hij->thj", query_block, rounded, preferred_element_type=jnp.float32
        )
        query_part = factor * jnp.einsum(
            "thj,hij->thi", grad_block, rounded, preferred_element_type=jnp.float32
        )
        return (carry_state, (result, query_part))

    def backward(carry_state, block):
        key_block, value_block, state_term = block
        carry_state = carry_state + state_term
        rounded = carry_state.astype(jnp.bfloat16)
        value_part = jnp.einsum(
            "thi,hij->thj", key_block, rounded, preferred_element_type=jnp.float32
        )
        key_part = jnp.einsum(
            "thj,hij->thi", value_block, rounded, preferred_element_type=jnp.float32
        )
        return (carry_state, (value_part, key_part))

    unused_a, (result, query_part) = lax.scan(
        forward, kv_before, (query_act, grad_rows, kv_each, row_scale)
    )
    unused_b, (value_part, key_part) = lax.scan(
        backward, grad_after, (key_act, value_rows, grad_each), reverse=True
    )
    attn_out = result.reshape(token_count, feature_width).astype(jnp.bfloat16)
    query_grad = jnp.where(
        query_pre > 0, query_part.reshape(token_count, feature_width), 0.0
    ).astype(jnp.bfloat16)
    key_grad = jnp.where(
        key_in.reshape(token_count, feature_width) > 0,
        key_part.reshape(token_count, feature_width),
        0.0,
    ).astype(jnp.bfloat16)
    value_grad = value_part.reshape(token_count, feature_width).astype(jnp.bfloat16)
    return (attn_out, query_grad, key_grad, value_grad)


def solution(mesh):
    return jax.shard_map(
        local,
        mesh=mesh,
        in_specs=(
            P(("grp", "group"), None),
            P(("grp", "group"), None),
            P(("grp", "group"), None),
            P(("grp", "group"), None),
            P(("grp", "group")),
            P(),
        ),
        out_specs=(
            P(("grp", "group"), None),
            P(("grp", "group"), None),
            P(("grp", "group"), None),
            P(("grp", "group"), None),
        ),
        check_vma=False,
    )
```

profile of v0, /device:TPU:29, one launch (start us, length us, event | category | flops | bytes accessed | tf_op | source)
XLA Modules:
  0.0 258.6 jit_solution(13105247291025714039)
XLA Ops:
  12.6 3.0 %fusion.28 = (f32[20,112,112]{2,1,0:T(8,128)}, f32[2,20,112,112]{3,2,1,0:T(8,128)}) fusion(bf16[2,64,20,112]{3,1,2,0:T(8,128)(2,1)S(1)} %copy.51, bf16[2,64,20,112]{3,1,2,0:T(8,128)(2,1)S(1)} %copy.52, f32[2]{0:T(128)S(1)} %multiply_divide_fusion), kind=kOutput, calls=%fused_computation.43 | convolution fusion | flops 64977920 | bytes 4157448 | tf_op jit(solution)/shard_map/cthi,cthj->chij/dot_general | solution.py:49
  19.8 1.9 copy.46
  21.7 2.7 %fusion.27 = (f32[20,112,112]{2,1,0:T(8,128)}, f32[2,20,112,112]{3,2,1,0:T(8,128)S(1)}) fusion(bf16[2,64,20,112]{3,1,2,0:T(8,128)(2,1)S(1)} %copy.45, bf16[2,64,20,112]{3,1,2,0:T(8,128)(2,1)} %copy.46), kind=kOutput, calls=%fused_computation.42 | convolution fusion | flops 64476160 | bytes 4157440 | tf_op jit(solution)/shard_map/cthi,cthj->chij/dot_general | solution.py:48
  24.5 88.3 %all-gather.7.cloned.1.call-done = f32[320,112,112]{2,1,0:T(8,128)} async-done(((f32[20,112,112]{2,1,0:T(8,128)}), f32[320,112,112]{2,1,0:T(8,128)}) %all-gather.7.cloned.1.call-update) | async-done | bytes 16056336 | tf_op jit(solution)/shard_map/all_gather | solution.py:18
  114.8 8.0 %while.57 = (s32[]{:T(128)}, f32[20,112,112]{2,1,0:T(8,128)S(1)}, bf16[2,64,20,112]{3,1,2,0:T(8,128)(2,1)}, bf16[2,64,20,112]{3,1,2,0:T(8,128)(2,1)}, f32[2,20,1...) while((s32[]{:T(128)}, f32[20,112,112]{2,1,0:T(8,128)S(1)}, ...), condition=%wide.region_9.10_spmd, body=%wide.region_8.9_spmd.sunk | while | flops 64977920 | bytes 16283861 | solution.py:85
  114.8 1.6 bitcast_add_fusion.12
  118.8 1.6 bitcast_add_fusion.12
  122.9 2.5 copy.62
  125.4 2.4 reshape.52
  130.1 2.5 copy.69
  132.6 1.4 reshape.57
  134.0 76.9 %all-gather.5.cloned.1.call-done = f32[320,112,112]{2,1,0:T(8,128)} async-done(((f32[20,112,112]{2,1,0:T(8,128)}), f32[320,112,112]{2,1,0:T(8,128)}) %all-gather.5.cloned.1.call-update) | async-done | bytes 16056336 | tf_op jit(solution)/shard_map/all_gather | solution.py:18
  210.9 23.1 %while.54 = (s32[]{:T(128)}, f32[20,112,112]{2,1,0:T(8,128)S(1)}, s32[]{:T(128)}, f32[16,20,112,112]{3,2,1,0:T(8,128)}, s32[]{:T(128)}, /*index=5*/s32[]{:T(128)}, s32[]{:T(128)}) while((s32[]{:T(128)}, f32[20,112,112]{2,1,0:T(8,128)S(1)}, s32[]{:T(128)}, f32[16,20,112,112]{3,2,1,0:T(8,128)}, s32[]{:T(128)}, /*index=5*/s32[]{:T(128)}, ...), condition=%wide.region_2.3_spmd, body=%wide.region_1.0_spmd.sunk | while | flops 250885 | bytes 3010675 | solution.py:25
  211.0 1.5 bitcast_add_fusion.9
  212.5 1.5 bitcast_add_fusion.9
  214.0 1.5 bitcast_add_fusion.9
  215.6 1.5 bitcast_add_fusion.9
  217.1 1.5 bitcast_add_fusion.9
  218.6 1.5 bitcast_add_fusion.9
  220.1 1.5 bitcast_add_fusion.9
  221.7 1.5 bitcast_add_fusion.9
  223.2 1.5 bitcast_add_fusion.9
  224.7 1.5 bitcast_add_fusion.9
  226.2 1.5 bitcast_add_fusion.9
  227.8 1.5 bitcast_add_fusion.9
  229.3 1.5 bitcast_add_fusion.9
  230.8 1.5 bitcast_add_fusion.9
  232.4 1.5 bitcast_add_fusion.9
  236.1 9.9 %while.55 = (s32[]{:T(128)}, f32[20,112,112]{2,1,0:T(8,128)S(1)}, bf16[2,64,20,112]{3,1,2,0:T(8,128)(2,1)}, bf16[2,64,20,112]{3,1,2,0:T(8,128)(2,1)}, f32[2,20,1...) while((s32[]{:T(128)}, f32[20,112,112]{2,1,0:T(8,128)S(1)}, ...), condition=%wide.region_4.5_spmd, body=%wide.region_3.4_spmd.sunk | while | flops 65264640 | bytes 16284893 | solution.py:82
  239.2 1.9 fusion.51
  244.1 1.9 fusion.51
  246.0 1.6 copy.55
  (102 shorter events, 30.9 us)
Async XLA Ops:
  7.2 10.6 %copy-start = (bf16[21,2240]{1,0:T(8,128)(2,1)S(1)}, bf16[21,2240]{1,0:T(8,128)(2,1)}, u32[]{:S(2)}) copy-start(bf16[21,2240]{1,0:T(8,128)(2,1)} %param.19) | copy-start | bytes 282244
  7.2 105.6 %all-gather.7.cloned.1.call-start = ((), (), s32[]{:S(2)}) async-start(), calls=%async_computation.1 | async-start | bytes 19496960 | tf_op jit(solution)/shard_map/all_gather | solution.py:18
  8.6 0.8 copy-start.9
  10.2 1.1 copy-start.19
  11.3 1.3 copy-start.4
  12.6 3.0 %copy-start.2 = (bf16[2,64,20,112]{3,1,2,0:T(8,128)(2,1)}, bf16[2,64,20,112]{3,1,2,0:T(8,128)(2,1)S(1)}, u32[]{:S(2)}) copy-start(bf16[2,64,20,112]{3,1,2,0:T(8,128)(2,1)S(1)} %copy.52) | copy-start | bytes 1720324
  15.7 1.1 copy-start.18
  15.7 195.2 %all-gather.5.cloned.1.call-start = ((), (), s32[]{:S(2)}) async-start(), calls=%async_computation | async-start | bytes 19496960 | tf_op jit(solution)/shard_map/all_gather | solution.py:18
  17.0 1.0 copy-start.11
  17.0 0.8 copy-start.21
  18.3 1.1 copy-start.20
  19.3 2.4 copy-start.6
  114.8 1.6 copy-start.7
  114.8 1.6 copy-start.16
  116.4 1.2 copy-start.8
  116.8 0.8 copy-start.17
  118.8 1.6 copy-start.7
  118.8 1.6 copy-start.16
  120.4 1.2 copy-start.8
  120.8 0.8 copy-start.17
  122.9 4.9 %copy-start.12 = (bf16[128,2240]{1,0:T(8,128)(2,1)S(1)}, bf16[128,2240]{1,0:T(8,128)(2,1)}, u32[]{:S(2)}) copy-start(bf16[128,2240]{1,0:T(8,128)(2,1)} %copy-done.11) | copy-start | bytes 1720324
  236.1 1.1 copy-start.5
  236.1 1.3 copy-start.13
  236.3 2.9 %copy-start.3 = (bf16[2,64,20,112]{3,1,2,0:T(8,128)(2,1)S(1)}, bf16[2,64,20,112]{3,1,2,0:T(8,128)(2,1)}, u32[]{:S(2)}) copy-start(bf16[2,64,20,112]{3,1,2,0:T(8,128)(2,1)} %get-tuple-element.560) | copy-start | bytes 1720324 | tf_op jit(solution)/shard_map/while
  238.3 0.8 copy-start.14
  241.0 1.1 copy-start.5
  241.0 1.3 copy-start.13
  241.3 2.9 %copy-start.3 = (bf16[2,64,20,112]{3,1,2,0:T(8,128)(2,1)S(1)}, bf16[2,64,20,112]{3,1,2,0:T(8,128)(2,1)}, u32[]{:S(2)}) copy-start(bf16[2,64,20,112]{3,1,2,0:T(8,128)(2,1)} %get-tuple-element.560) | copy-start | bytes 1720324 | tf_op jit(solution)/shard_map/while
  243.3 0.8 copy-start.14
  246.0 2.2 copy-start.10
  248.2 1.2 copy-start.15
  249.5 2.3 copy-start.1
Sparse Core Ops, SparseCore 0:
  15.8 96.8 all-gather.6
  114.4 96.4 all-gather.4
where the time goes:
time: 260 us; the launch traced here: 259 us
  waiting for transfers between devices  165 us (63%)
  local copies, waits for them, and re-layouts  35.7 us (14%)
  other arithmetic  27.8 us (11%)
  matrix products  14.7 us (6%)
  between operations  14.3 us (6%)
    all_gather x2, waiting for transfers between devices, prefix(): gathered = lax.all_gather(part, axis)  165 us
    add x15, other arithmetic, add_pair(): return earlier + later  22.5 us
    unnamed x36, local copies, waits for them, and re-layouts  13.3 us
  transfers between devices with their start and end apart: 2, of which 2 were waited for; matrix products, arithmetic and copies ran while one was open for 10% of the time, Pallas kernels for 0%

commit v1 on v0

v1 whole, which is shorter than its diff:
```python
import functools

import jax
import jax.numpy as jnp
from jax import lax
from jax.experimental import pallas as pl
from jax.experimental.pallas import tpu as pltpu
from jax.sharding import PartitionSpec as P

HEADS = 20
HD = 112
CL = 64
CHUNK = 384
HALF = HD // 2

score_scale = 4.0
MESH = pl.DeviceIdType.MESH
F32 = jnp.float32
BF16 = jnp.bfloat16


def dot(a, b, dims):
    return lax.dot_general(a, b, (dims, ((), ())), preferred_element_type=F32)


def kernel(n, width, q_ref, k_ref, v_ref, g_ref, frame_ref, embed_ref,
           out_ref, qg_ref, kg_ref, vg_ref,
           act, total, first, sib_in, chip, pair_in, chain_in, chain_out,
           pair_out, prefix, sib_out, send_sem, recv_sem):
    packed = total.shape[2]
    chunks = packed // CHUNK
    me = lax.axis_index("group")
    core = lax.rem(me, 2)
    mid = lax.rem(me // 2, 2)
    outer = me // 4
    depth = n // 4
    place = outer + core * (depth - 1 - 2 * outer)
    has_prev = place > 0
    has_next = place < depth - 1
    lead = mid == core
    sibling = me + 1 - 2 * core
    partner = me + 2 - 4 * mid
    onward = lax.rem(me + 4 - 8 * core + n, n)
    back = lax.rem(me - 4 + 8 * core + n, n)
    mine = pl.ds(pl.multiple_of(HALF * mid, 8), HALF)
    other = pl.ds(pl.multiple_of(HALF * (1 - mid), 8), HALF)

    barrier = pltpu.get_barrier_semaphore()
    for peer in (sibling, partner, onward, back):
        pl.semaphore_signal(barrier, inc=1, device_id={"group": peer}, device_id_type=MESH)

    def lanes(k):
        return pl.ds(k * CHUNK, CHUNK)

    def copy(phase, k, src, dst, peer):
        return pltpu.make_async_remote_copy(
            src_ref=src, dst_ref=dst, send_sem=send_sem.at[phase, k],
            recv_sem=recv_sem.at[phase, k], device_id={"group": peer}, device_id_type=MESH)

    def sib_first(k):
        return copy(0, k, total.at[1 - core, :, lanes(k)], sib_in.at[:, lanes(k)], sibling)

    def pair_first(k):
        return copy(1, k, chip.at[other, lanes(k)], pair_in.at[:, lanes(k)], partner)

    def chain(k):
        return copy(2, k, chain_out.at[:, lanes(k)], chain_in.at[:, lanes(k)], onward)

    def pair_last(k):
        return copy(3, k, pair_out.at[:, lanes(k)], prefix.at[core, mine, lanes(k)], partner)

    def sib_last(k):
        return copy(4, k, sib_out.at[:, lanes(k)], prefix.at[core, :, lanes(k)], sibling)

    scales = []
    for b in range(2):
        tokens = (me * 2 + b + 1) * CL
        scales.append(score_scale / (HD * jnp.sqrt(jnp.full((1, HD), tokens, jnp.int32).astype(F32))))

    for kind in range(2):
        total[kind, :, packed - 128:] = jnp.zeros((HD, 128), F32)
    ids = lax.broadcasted_iota(jnp.int32, (CL, embed_ref.shape[0]), 1)
    for b in range(2):
        onehot = jnp.where(ids == frame_ref[b], 1.0, 0.0).astype(BF16)
        rows = slice(CL * b, CL * b + CL)
        for k in range(chunks):
            cols = slice(k * CHUNK, min(k * CHUNK + CHUNK, width))
            shift = dot(onehot, embed_ref[:, cols], ((1,), (0,)))
            act[rows, cols] = jnp.maximum(k_ref[rows, cols].astype(F32) + shift, 0.0).astype(BF16)

    def head_state(h):
        cols = slice(h * HD, h * HD + HD)
        key, value, grad = act[:, cols], v_ref[:, cols], g_ref[:, cols]
        query = jnp.maximum(q_ref[:, cols], 0)
        early, late = slice(0, CL), slice(CL, 2 * CL)
        tn = ((0,), (0,))
        kv0 = dot(key[early], value[early], tn)
        kv1 = dot(key[late], value[late], tn)
        first[0, :, cols] = kv0
        total[0, :, cols] = kv0 + kv1
        gr0 = scales[0] * dot(query[early], grad[early], tn)
        gr1 = scales[1] * dot(query[late], grad[late], tn)
        first[1, :, cols] = gr1
        total[1, :, cols] = gr0 + gr1

    done = [0]

    def stage_a(k):
        while done[0] < HEADS and done[0] * HD < (k + 1) * CHUNK:
            head_state(done[0])
            done[0] += 1
        if k == 0:
            pl.semaphore_wait(barrier, 4)
        sib_first(k).start()

    def stage_b(k):
        sib_first(k).wait_recv()
        chip[:, lanes(k)] = total[core, :, lanes(k)] + sib_in[:, lanes(k)]
        pair_first(k).start()

    def stage_c(k):
        @pl.when(has_prev)
        def _():
            chain(k).wait_recv()

        @pl.when(jnp.logical_not(has_prev))
        def _():
            chain_in[:, lanes(k)] = jnp.zeros((HALF, CHUNK), F32)

        pair_first(k).wait_recv()

        @pl.when(has_next)
        def _():
            chain_out[:, lanes(k)] = chain_in[:, lanes(k)] + (chip[mine, lanes(k)] + pair_in[:, lanes(k)])
            chain(k).start()

        @pl.when(lead)
        def _():
            pair_out[:, lanes(k)] = chain_in[:, lanes(k)] + chip[mine, lanes(k)]
            prefix[core, mine, lanes(k)] = chain_in[:, lanes(k)]

        @pl.when(jnp.logical_not(lead))
        def _():
            pair_out[:, lanes(k)] = chain_in[:, lanes(k)]
            prefix[core, mine, lanes(k)] = chain_in[:, lanes(k)] + pair_in[:, lanes(k)]

        pair_last(k).start()

    def stage_d(k):
        pair_last(k).wait_recv()
        sib_out[:, lanes(k)] = prefix[core, :, lanes(k)] + total[core, :, lanes(k)]
        sib_last(k).start()

    def head_out(h):
        cols = slice(h * HD, h * HD + HD)
        before, after = prefix[0, :, cols], prefix[1, :, cols]
        kv = [(before + first[0, :, cols]).astype(BF16), (before + total[0, :, cols]).astype(BF16)]
        gr = [(after + total[1, :, cols]).astype(BF16), (after + first[1, :, cols]).astype(BF16)]
        nn, nt = ((1,), (0,)), ((1,), (1,))
        for b in range(2):
            rows = slice(CL * b, CL * b + CL)
            query = jnp.maximum(q_ref[rows, cols], 0)
            key, value, grad = act[rows, cols], v_ref[rows, cols], g_ref[rows, cols]
            out_ref[rows, cols] = (scales[b] * dot(query, kv[b], nn)).astype(BF16)
            part = scales[b] * dot(grad, kv[b], nt)
            qg_ref[rows, cols] = jnp.where(query.astype(F32) > 0, part, 0.0).astype(BF16)
            vg_ref[rows, cols] = dot(key, gr[b], nn).astype(BF16)
            part = dot(value, gr[b], nt)
            kg_ref[rows, cols] = jnp.where(key.astype(F32) > 0, part, 0.0).astype(BF16)

    written = [0]

    def stage_e(k):
        sib_last(k).wait_recv()
        while written[0] < HEADS and (written[0] + 1) * HD <= (k + 1) * CHUNK:
            head_out(written[0])
            written[0] += 1

    order = []
    for k in range(chunks + 1):
        order += [(stage_a, k), (stage_b, k - 1)]
    for k in range(chunks + 4):
        order += [(stage_c, k), (stage_d, k - 2), (stage_e, k - 4)]
    for stage, k in order:
        if 0 <= k < chunks:
            stage(k)

    for k in range(chunks):
        sib_first(k).wait_send()
        pair_first(k).wait_send()
        pair_last(k).wait_send()
        sib_last(k).wait_send()

    @pl.when(has_next)
    def _():
        for k in range(chunks):
            chain(k).wait_send()


def local(query_pre, key_pre, values, out_grad, block_frame, frame_embed):
    n = lax.axis_size("group")
    rows, width = query_pre.shape
    packed = -(-width // CHUNK) * CHUNK
    chunks = packed // CHUNK
    vmem = pl.BlockSpec(memory_space=pltpu.VMEM)
    result = jax.ShapeDtypeStruct((rows, width), BF16)
    return pl.pallas_call(
        functools.partial(kernel, n, width),
        out_shape=(result,) * 4,
        in_specs=[vmem] * 4 + [pl.BlockSpec(memory_space=pltpu.SMEM), vmem],
        out_specs=(vmem,) * 4,
        scratch_shapes=[
            pltpu.VMEM((rows, width), BF16),
            pltpu.VMEM((2, HD, packed), F32),
            pltpu.VMEM((2, HD, packed), F32),
            pltpu.VMEM((HD, packed), F32),
            pltpu.VMEM((HD, packed), F32),
            pltpu.VMEM((HALF, packed), F32),
            pltpu.VMEM((HALF, packed), F32),
            pltpu.VMEM((HALF, packed), F32),
            pltpu.VMEM((HALF, packed), F32),
            pltpu.VMEM((2, HD, packed), F32),
            pltpu.VMEM((HD, packed), F32),
            pltpu.SemaphoreType.DMA((5, chunks)),
            pltpu.SemaphoreType.DMA((5, chunks)),
        ],
        compiler_params=pltpu.CompilerParams(
            collective_id=0, has_side_effects=True, vmem_limit_bytes=44 * 1024 * 1024),
    )(query_pre, key_pre, values, out_grad, block_frame, frame_embed)


def solution(mesh):
    rows = P(("grp", "group"), None)
    return jax.shard_map(
        local,
        mesh=mesh,
        in_specs=(rows, rows, rows, rows, P(("grp", "group")), P()),
        out_specs=(rows,) * 4,
        check_vma=False,
    )
```

time: 260 us -> 53.6 us (0.21)
  the two profiles are of different devices: /device:TPU:29 before, /device:TPU:1 now
where the time goes in v1:
time: 53.6 us; the launch traced here: 53.3 us
  Pallas kernels  40.7 us (76%)
  local copies, waits for them, and re-layouts  12 us (22%)
  between operations  0.69 us (1%)
    pallas_call x1, Pallas kernels, local(): pl.pallas_call(functools.partial(kernel, n, width), out_shape=(result,) *...  40.7 us
    unnamed x20, local copies, waits for them, and re-layouts  6.65 us
    pallas_call x4, local copies, waits for them, and re-layouts, local(): pl.pallas_call(functools.partial(kernel, n, width), out_shape=(result,) *...  5.31 us

profile of v1, /device:TPU:1, one launch (start us, length us, event | category | flops | bytes accessed | tf_op | source)
XLA Modules:
  0.0 53.3 jit_solution(13324096275502623161)
XLA Ops:
  0.6 0.0 copy-start.5
  0.6 1.4 %copy.10.q_ref = bf16[128,2240]{1,0:T(8,128)(2,1)S(1)} copy(bf16[128,2240]{0,1:T(8,128)(2,1)} %param.6) | data formatting | bytes 1146880 | tf_op args[0]
  2.0 0.0 copy-done.5
  2.0 0.0 copy-start.6
  2.0 0.2 copy.11.k_ref
  2.3 0.8 %copy-done.6 = bf16[128,2240]{0,1:T(8,128)(2,1)S(1)} copy-done((bf16[128,2240]{0,1:T(8,128)(2,1)S(1)}, bf16[128,2240]{0,1:T(8,128)(2,1)}, u32[]{:S(2)}) %copy-start.6) | copy-done | bytes 573464
  3.1 0.0 copy-start.7
  3.1 0.2 copy.12.v_ref
  3.3 0.8 %copy-done.7 = bf16[128,2240]{0,1:T(8,128)(2,1)S(1)} copy-done((bf16[128,2240]{0,1:T(8,128)(2,1)S(1)}, bf16[128,2240]{0,1:T(8,128)(2,1)}, u32[]{:S(2)}) %copy-start.7) | copy-done | bytes 573464
  4.1 0.0 copy-start.4
  4.1 0.2 copy.13.g_ref
  4.4 0.4 copy-done.4
  4.8 0.0 copy-start.3
  4.8 0.9 %copy-done.3 = bf16[21,2240]{1,0:T(8,128)(2,1)S(1)} copy-done((bf16[21,2240]{1,0:T(8,128)(2,1)S(1)}, bf16[21,2240]{1,0:T(8,128)(2,1)}, u32[]{:S(2)}) %copy-start.3) | copy-done | bytes 94104
  5.7 40.7 %shard_map.93 = (bf16[128,2240]{1,0:T(8,128)(2,1)S(1)}, bf16[128,2240]{1,0:T(8,128)(2,1)S(1)}, bf16[128,2240]{1,0:T(8,128)(2,1)S(1)}, bf16[128,2240]{1,0:T(8,128)(2,1)S(1)}) custom-call(bf16[128,2240]{1,0:T(8,128)(2,1)S(1)} %copy.10.q_ref, bf16[128,2240]{1,0:T(8,128)(2,1)S(1)} %copy.11.k_ref, bf16[128,2240]{1,0:T(8,128)(2,1)S(1)} %copy.12.v_ref, ...), custom_call_target="tpu_custom_call" | custom-call | tf_op jit(solution)/shard_map/pallas_call | solution.py:207
  46.4 0.0 copy-start
  46.4 0.8 %copy-done = bf16[128,2240]{1,0:T(8,128)(2,1)} copy-done((bf16[128,2240]{1,0:T(8,128)(2,1)}, bf16[128,2240]{1,0:T(8,128)(2,1)S(1)}, u32[]{:S(2)}) %copy-start) | copy-done | bytes 573464
  47.2 0.0 copy-start.2
  47.2 0.8 %copy-done.2 = bf16[128,2240]{1,0:T(8,128)(2,1)} copy-done((bf16[128,2240]{1,0:T(8,128)(2,1)}, bf16[128,2240]{1,0:T(8,128)(2,1)S(1)}, u32[]{:S(2)}) %copy-start.2) | copy-done | bytes 573464
  48.0 0.0 copy-start.1
  48.0 2.2 %copy.14 = bf16[128,2240]{0,1:T(8,128)(2,1)} copy(bf16[128,2240]{1,0:T(8,128)(2,1)} %copy-done.2) | data formatting | bytes 1146880 | tf_op jit(solution)/shard_map/pallas_call | solution.py:207
  50.2 0.0 copy-done.1
  50.2 1.0 %copy.15 = bf16[128,2240]{0,1:T(8,128)(2,1)} copy(bf16[128,2240]{1,0:T(8,128)(2,1)S(1)} %copy-done.1) | data formatting | bytes 1146880 | tf_op jit(solution)/shard_map/pallas_call | solution.py:207
  51.2 1.0 %copy.16 = bf16[128,2240]{0,1:T(8,128)(2,1)} copy(bf16[128,2240]{1,0:T(8,128)(2,1)S(1)} %get-tuple-element.6) | data formatting | bytes 1146880 | tf_op jit(solution)/shard_map/pallas_call | solution.py:207
  52.3 1.0 %copy.17 = bf16[128,2240]{0,1:T(8,128)(2,1)} copy(bf16[128,2240]{1,0:T(8,128)(2,1)S(1)} %get-tuple-element.7) | data formatting | bytes 1146880 | tf_op jit(solution)/shard_map/pallas_call | solution.py:207
Async XLA Ops:
  0.6 1.4 %copy-start.5 = (bf16[128,2240]{0,1:T(8,128)(2,1)S(1)}, bf16[128,2240]{0,1:T(8,128)(2,1)}, u32[]{:S(2)}) copy-start(bf16[128,2240]{0,1:T(8,128)(2,1)} %param.7) | copy-start | bytes 1720324
  2.0 1.1 %copy-start.6 = (bf16[128,2240]{0,1:T(8,128)(2,1)S(1)}, bf16[128,2240]{0,1:T(8,128)(2,1)}, u32[]{:S(2)}) copy-start(bf16[128,2240]{0,1:T(8,128)(2,1)} %param.8) | copy-start | bytes 1720324
  3.1 1.1 %copy-start.7 = (bf16[128,2240]{0,1:T(8,128)(2,1)S(1)}, bf16[128,2240]{0,1:T(8,128)(2,1)}, u32[]{:S(2)}) copy-start(bf16[128,2240]{0,1:T(8,128)(2,1)} %param.9) | copy-start | bytes 1720324
  4.1 0.7 %copy-start.4 = (s32[2]{0:T(128)S(1)}, s32[2]{0:T(128)}, u32[]{:S(2)}) copy-start(s32[2]{0:T(128)} %frame_ref.1) | copy-start | bytes 28
  4.8 0.9 %copy-start.3 = (bf16[21,2240]{1,0:T(8,128)(2,1)S(1)}, bf16[21,2240]{1,0:T(8,128)(2,1)}, u32[]{:S(2)}) copy-start(bf16[21,2240]{1,0:T(8,128)(2,1)} %embed_ref.1) | copy-start | bytes 282244
  46.4 0.8 %copy-start = (bf16[128,2240]{1,0:T(8,128)(2,1)}, bf16[128,2240]{1,0:T(8,128)(2,1)S(1)}, u32[]{:S(2)}) copy-start(bf16[128,2240]{1,0:T(8,128)(2,1)S(1)} %get-tuple-element.5) | copy-start | bytes 1720324
  47.2 0.8 %copy-start.2 = (bf16[128,2240]{1,0:T(8,128)(2,1)}, bf16[128,2240]{1,0:T(8,128)(2,1)S(1)}, u32[]{:S(2)}) copy-start(bf16[128,2240]{1,0:T(8,128)(2,1)S(1)} %get-tuple-element.4) | copy-start | bytes 1720324
  48.0 2.2 %copy-start.1 = (bf16[128,2240]{1,0:T(8,128)(2,1)S(1)}, bf16[128,2240]{1,0:T(8,128)(2,1)}, u32[]{:S(2)}) copy-start(bf16[128,2240]{1,0:T(8,128)(2,1)} %copy-done) | copy-start | bytes 1720324

commit v2 on v1

--- a/solution.py
+++ b/solution.py
@@ -25,7 +25,7 @@
 
 def kernel(n, width, q_ref, k_ref, v_ref, g_ref, frame_ref, embed_ref,
            out_ref, qg_ref, kg_ref, vg_ref,
-           act, total, first, sib_in, chip, pair_in, chain_in, chain_out,
+           act, total, first, local_sum, sib_in, chip, pair_in, chain_in, chain_out,
            pair_out, prefix, sib_out, send_sem, recv_sem):
     packed = total.shape[2]
     chunks = packed // CHUNK
@@ -72,36 +72,49 @@
     def sib_last(k):
         return copy(4, k, sib_out.at[:, lanes(k)], prefix.at[core, :, lanes(k)], sibling)
 
-    scales = []
+    lane = lax.broadcasted_iota(jnp.int32, (1, 2 * CL), 1)
+    early = lane < CL
+    tokens = jnp.where(early, me * 2 + 1, me * 2 + 2) * CL
+    scale = score_scale / (HD * jnp.sqrt(tokens.astype(F32)))
+    state_scales = []
     for b in range(2):
-        tokens = (me * 2 + b + 1) * CL
-        scales.append(score_scale / (HD * jnp.sqrt(jnp.full((1, HD), tokens, jnp.int32).astype(F32))))
+        tokens = jnp.full((1, HD), (me * 2 + b + 1) * CL, jnp.int32)
+        state_scales.append(score_scale / (HD * jnp.sqrt(tokens.astype(F32))))
+    masks = [early.astype(F32).astype(BF16), (lane >= CL).astype(F32).astype(BF16)]
 
     for kind in range(2):
         total[kind, :, packed - 128:] = jnp.zeros((HD, 128), F32)
-    ids = lax.broadcasted_iota(jnp.int32, (CL, embed_ref.shape[0]), 1)
-    for b in range(2):
-        onehot = jnp.where(ids == frame_ref[b], 1.0, 0.0).astype(BF16)
-        rows = slice(CL * b, CL * b + CL)
-        for k in range(chunks):
-            cols = slice(k * CHUNK, min(k * CHUNK + CHUNK, width))
-            shift = dot(onehot, embed_ref[:, cols], ((1,), (0,)))
-            act[rows, cols] = jnp.maximum(k_ref[rows, cols].astype(F32) + shift, 0.0).astype(BF16)
+    frames = embed_ref.shape[0]
+    ids = lax.broadcasted_iota(jnp.int32, (frames, 2 * CL), 0)
+    block = lax.broadcasted_iota(jnp.int32, (frames, 2 * CL), 1) < CL
+    onehot = jnp.where(ids == jnp.where(block, frame_ref[0], frame_ref[1]), 1.0, 0.0).astype(BF16)
+    acted = [0]
+
+    def act_until(end):
+        while acted[0] < end:
+            part = slice(acted[0], min(acted[0] + CHUNK, width))
+            shift = dot(embed_ref[:, part], onehot, ((0,), (0,)))
+            act[part] = jnp.maximum(k_ref[part].astype(F32) + shift, 0.0).astype(BF16)
+            acted[0] = part.stop
+
+    def split(x):
+        return jnp.concatenate([x * masks[0], x * masks[1]], axis=0)
 
     def head_state(h):
-        cols = slice(h * HD, h * HD + HD)
-        key, value, grad = act[:, cols], v_ref[:, cols], g_ref[:, cols]
-        query = jnp.maximum(q_ref[:, cols], 0)
-        early, late = slice(0, CL), slice(CL, 2 * CL)
-        tn = ((0,), (0,))
-        kv0 = dot(key[early], value[early], tn)
-        kv1 = dot(key[late], value[late], tn)
-        first[0, :, cols] = kv0
-        total[0, :, cols] = kv0 + kv1
-        gr0 = scales[0] * dot(query[early], grad[early], tn)
-        gr1 = scales[1] * dot(query[late], grad[late], tn)
-        first[1, :, cols] = gr1
-        total[1, :, cols] = gr0 + gr1
+        part = slice(h * HD, h * HD + HD)
+        act_until(part.stop)
+        nt = ((1,), (1,))
+        both = dot(split(act[part]), v_ref[part], nt)
+        first[0, h] = both[:HD]
+        both = both[:HD] + both[HD:]
+        local_sum[0, h] = both
+        total[0, :, part] = both
+        both = dot(split(jnp.maximum(q_ref[part], 0)), g_ref[part], nt)
+        late = state_scales[1] * both[HD:]
+        first[1, h] = late
+        both = state_scales[0] * both[:HD] + late
+        local_sum[1, h] = both
+        total[1, :, part] = both
 
     done = [0]
 
@@ -152,21 +165,22 @@
         sib_last(k).start()
 
     def head_out(h):
-        cols = slice(h * HD, h * HD + HD)
-        before, after = prefix[0, :, cols], prefix[1, :, cols]
-        kv = [(before + first[0, :, cols]).astype(BF16), (before + total[0, :, cols]).astype(BF16)]
-        gr = [(after + total[1, :, cols]).astype(BF16), (after + first[1, :, cols]).astype(BF16)]
-        nn, nt = ((1,), (0,)), ((1,), (1,))
-        for b in range(2):
-            rows = slice(CL * b, CL * b + CL)
-            query = jnp.maximum(q_ref[rows, cols], 0)
-            key, value, grad = act[rows, cols], v_ref[rows, cols], g_ref[rows, cols]
-            out_ref[rows, cols] = (scales[b] * dot(query, kv[b], nn)).astype(BF16)
-            part = scales[b] * dot(grad, kv[b], nt)
-            qg_ref[rows, cols] = jnp.where(query.astype(F32) > 0, part, 0.0).astype(BF16)
-            vg_ref[rows, cols] = dot(key, gr[b], nn).astype(BF16)
-            part = dot(value, gr[b], nt)
-            kg_ref[rows, cols] = jnp.where(key.astype(F32) > 0, part, 0.0).astype(BF16)
+        part = slice(h * HD, h * HD + HD)
+        nn, tn = ((1,), (0,)), ((0,), (0,))
+        query = jnp.maximum(q_ref[part], 0)
+        key = act[part]
+        before = prefix[0, :, part]
+        state = jnp.concatenate([(before + first[0, h]).astype(BF16), (before + local_sum[0, h]).astype(BF16)], axis=0)
+        out_ref[part] = (scale * dot(state, split(query), tn)).astype(BF16)
+        both = dot(state, g_ref[part], nn)
+        both = scale * jnp.where(early, both[:HD], both[HD:])
+        qg_ref[part] = jnp.where(query.astype(F32) > 0, both, 0.0).astype(BF16)
+        after = prefix[1, :, part]
+        state = jnp.concatenate([(after + local_sum[1, h]).astype(BF16), (after + first[1, h]).astype(BF16)], axis=0)
+        vg_ref[part] = dot(state, split(key), tn).astype(BF16)
+        both = dot(state, v_ref[part], nn)
+        both = jnp.where(early, both[:HD], both[HD:])
+        kg_ref[part] = jnp.where(key.astype(F32) > 0, both, 0.0).astype(BF16)
 
     written = [0]
 
@@ -203,16 +217,17 @@
     packed = -(-width // CHUNK) * CHUNK
     chunks = packed // CHUNK
     vmem = pl.BlockSpec(memory_space=pltpu.VMEM)
-    result = jax.ShapeDtypeStruct((rows, width), BF16)
-    return pl.pallas_call(
+    result = jax.ShapeDtypeStruct((width, rows), BF16)
+    outs = pl.pallas_call(
         functools.partial(kernel, n, width),
         out_shape=(result,) * 4,
         in_specs=[vmem] * 4 + [pl.BlockSpec(memory_space=pltpu.SMEM), vmem],
         out_specs=(vmem,) * 4,
         scratch_shapes=[
-            pltpu.VMEM((rows, width), BF16),
+            pltpu.VMEM((width, rows), BF16),
             pltpu.VMEM((2, HD, packed), F32),
-            pltpu.VMEM((2, HD, packed), F32),
+            pltpu.VMEM((2, HEADS, HD, HD), F32),
+            pltpu.VMEM((2, HEADS, HD, HD), F32),
             pltpu.VMEM((HD, packed), F32),
             pltpu.VMEM((HD, packed), F32),
             pltpu.VMEM((HALF, packed), F32),
@@ -226,7 +241,8 @@
         ],
         compiler_params=pltpu.CompilerParams(
             collective_id=0, has_side_effects=True, vmem_limit_bytes=44 * 1024 * 1024),
-    )(query_pre, key_pre, values, out_grad, block_frame, frame_embed)
+    )(query_pre.T, key_pre.T, values.T, out_grad.T, block_frame, frame_embed)
+    return tuple(out.T for out in outs)
 
 
 def solution(mesh):

time: 53.6 us -> 50.8 us (0.948)
  local copies, waits for them, and re-layouts: 12 us -> 9.02 us
    pallas_call x4 -> x0, local copies, waits for them, and re-layouts: 5.31 us -> none  [local(): pl.pallas_call(functools.partial(kernel, n, width), out_shape=(result,) *...]
    unnamed x20 -> x16, local copies, waits for them, and re-layouts: 6.65 us -> 9.02 us
where the time goes in v2:
time: 50.8 us; the launch traced here: 50.5 us
  Pallas kernels  40.8 us (80%)
  local copies, waits for them, and re-layouts  9.02 us (18%)
  between operations  0.66 us (1%)
    pallas_call x1, Pallas kernels, local(): pl.pallas_call(functools.partial(kernel, n, width), out_shape=(result,) *...  40.8 us
    unnamed x16, local copies, waits for them, and re-layouts  9.02 us

profile of v2, /device:TPU:1, one launch (start us, length us, event | category | flops | bytes accessed | tf_op | source)
XLA Modules:
  0.0 50.5 jit_solution(18075232419996108238)
XLA Ops:
  0.6 0.0 copy-start.5
  0.6 0.6 %copy-done.5 = s32[2]{0:T(128)S(1)} copy-done((s32[2]{0:T(128)S(1)}, s32[2]{0:T(128)}, u32[]{:S(2)}) %copy-start.5) | copy-done | bytes 32
  1.3 0.0 copy-start
  1.3 1.1 %copy-done = bf16[128,2240]{0,1:T(8,128)(2,1)S(1)} copy-done((bf16[128,2240]{0,1:T(8,128)(2,1)S(1)}, bf16[128,2240]{0,1:T(8,128)(2,1)}, u32[]{:S(2)}) %copy-start) | copy-done | bytes 573464
  2.3 0.0 copy-start.1
  2.4 1.1 %copy-done.1 = bf16[128,2240]{0,1:T(8,128)(2,1)S(1)} copy-done((bf16[128,2240]{0,1:T(8,128)(2,1)S(1)}, bf16[128,2240]{0,1:T(8,128)(2,1)}, u32[]{:S(2)}) %copy-start.1) | copy-done | bytes 573464
  3.4 0.0 copy-start.2
  3.4 1.1 %copy-done.2 = bf16[128,2240]{0,1:T(8,128)(2,1)S(1)} copy-done((bf16[128,2240]{0,1:T(8,128)(2,1)S(1)}, bf16[128,2240]{0,1:T(8,128)(2,1)}, u32[]{:S(2)}) %copy-start.2) | copy-done | bytes 573464
  4.5 0.0 copy-start.3
  4.5 1.1 %copy-done.3 = bf16[128,2240]{0,1:T(8,128)(2,1)S(1)} copy-done((bf16[128,2240]{0,1:T(8,128)(2,1)S(1)}, bf16[128,2240]{0,1:T(8,128)(2,1)}, u32[]{:S(2)}) %copy-start.3) | copy-done | bytes 573464
  5.5 0.0 copy-start.4
  5.5 0.9 %copy-done.4 = bf16[21,2240]{1,0:T(8,128)(2,1)S(1)} copy-done((bf16[21,2240]{1,0:T(8,128)(2,1)S(1)}, bf16[21,2240]{1,0:T(8,128)(2,1)}, u32[]{:S(2)}) %copy-start.4) | copy-done | bytes 94104
  6.4 40.8 %shard_map.93 = (bf16[2240,128]{1,0:T(8,128)(2,1)S(1)}, bf16[2240,128]{1,0:T(8,128)(2,1)S(1)}, bf16[2240,128]{1,0:T(8,128)(2,1)S(1)}, bf16[2240,128]{1,0:T(8,128)(2,1)S(1)}) custom-call(bf16[2240,128]{1,0:T(8,128)(2,1)S(1)} %bitcast.8, bf16[2240,128]{1,0:T(8,128)(2,1)S(1)} %bitcast.9, bf16[2240,128]{1,0:T(8,128)(2,1)S(1)} %bitcast.10, ...), custom_call_target="tpu_custom_call" | custom-call | tf_op jit(solution)/shard_map/pallas_call | solution.py:221
  47.3 0.8 %copy.14 = bf16[128,2240]{0,1:T(8,128)(2,1)} copy(bf16[128,2240]{0,1:T(8,128)(2,1)S(1)} %bitcast.15) | data formatting | bytes 1146880
  48.1 0.8 %copy.15 = bf16[128,2240]{0,1:T(8,128)(2,1)} copy(bf16[128,2240]{0,1:T(8,128)(2,1)S(1)} %bitcast.14) | data formatting | bytes 1146880
  48.9 0.8 %copy.16 = bf16[128,2240]{0,1:T(8,128)(2,1)} copy(bf16[128,2240]{0,1:T(8,128)(2,1)S(1)} %bitcast.13) | data formatting | bytes 1146880
  49.7 0.8 %copy.17 = bf16[128,2240]{0,1:T(8,128)(2,1)} copy(bf16[128,2240]{0,1:T(8,128)(2,1)S(1)} %bitcast.12) | data formatting | bytes 1146880
Async XLA Ops:
  0.6 0.7 %copy-start.5 = (s32[2]{0:T(128)S(1)}, s32[2]{0:T(128)}, u32[]{:S(2)}) copy-start(s32[2]{0:T(128)} %frame_ref.1) | copy-start | bytes 28
  1.3 1.1 %copy-start = (bf16[128,2240]{0,1:T(8,128)(2,1)S(1)}, bf16[128,2240]{0,1:T(8,128)(2,1)}, u32[]{:S(2)}) copy-start(bf16[128,2240]{0,1:T(8,128)(2,1)} %param.6) | copy-start | bytes 1720324
  2.3 1.1 %copy-start.1 = (bf16[128,2240]{0,1:T(8,128)(2,1)S(1)}, bf16[128,2240]{0,1:T(8,128)(2,1)}, u32[]{:S(2)}) copy-start(bf16[128,2240]{0,1:T(8,128)(2,1)} %param.7) | copy-start | bytes 1720324
  3.4 1.1 %copy-start.2 = (bf16[128,2240]{0,1:T(8,128)(2,1)S(1)}, bf16[128,2240]{0,1:T(8,128)(2,1)}, u32[]{:S(2)}) copy-start(bf16[128,2240]{0,1:T(8,128)(2,1)} %param.8) | copy-start | bytes 1720324
  4.5 1.1 %copy-start.3 = (bf16[128,2240]{0,1:T(8,128)(2,1)S(1)}, bf16[128,2240]{0,1:T(8,128)(2,1)}, u32[]{:S(2)}) copy-start(bf16[128,2240]{0,1:T(8,128)(2,1)} %param.9) | copy-start | bytes 1720324
  5.5 0.9 %copy-start.4 = (bf16[21,2240]{1,0:T(8,128)(2,1)S(1)}, bf16[21,2240]{1,0:T(8,128)(2,1)}, u32[]{:S(2)}) copy-start(bf16[21,2240]{1,0:T(8,128)(2,1)} %embed_ref.1) | copy-start | bytes 282244

commit v3 on v2

--- a/solution.py
+++ b/solution.py
@@ -12,6 +12,7 @@
 CL = 64
 CHUNK = 384
 HALF = HD // 2
+PIECES = 2
 
 score_scale = 4.0
 MESH = pl.DeviceIdType.MESH
@@ -23,9 +24,10 @@
     return lax.dot_general(a, b, (dims, ((), ())), preferred_element_type=F32)
 
 
-def kernel(n, width, q_ref, k_ref, v_ref, g_ref, frame_ref, embed_ref,
-           out_ref, qg_ref, kg_ref, vg_ref,
-           act, total, first, local_sum, sib_in, chip, pair_in, chain_in, chain_out,
+def kernel(n, width, q_hbm, k_hbm, v_hbm, g_hbm, frame_hbm, embed_hbm,
+           out_hbm, qg_hbm, kg_hbm, vg_hbm,
+           out_ref, qg_ref, kg_ref, vg_ref, store_sem,
+           q_ref, k_ref, v_ref, g_ref, frame_ref, embed_ref, load_sem, small_sem, act, total, first, local_sum, sib_in, chip, pair_in, chain_in, chain_out,
            pair_out, prefix, sib_out, send_sem, recv_sem):
     packed = total.shape[2]
     chunks = packed // CHUNK
@@ -49,6 +51,19 @@
     for peer in (sibling, partner, onward, back):
         pl.semaphore_signal(barrier, inc=1, device_id={"group": peer}, device_id_type=MESH)
 
+    def load(k, which):
+        src, dst = ((k_hbm, k_ref), (v_hbm, v_ref), (q_hbm, q_ref), (g_hbm, g_ref))[which]
+        part = pl.ds(k * CHUNK, min(CHUNK, width - k * CHUNK))
+        return pltpu.make_async_copy(src.at[part], dst.at[part], load_sem.at[which, k])
+
+    small = [pltpu.make_async_copy(frame_hbm, frame_ref, small_sem.at[0]),
+             pltpu.make_async_copy(embed_hbm, embed_ref, small_sem.at[1])]
+    for one in small:
+        one.start()
+    for k in range(chunks):
+        for which in range(4):
+            load(k, which).start()
+
     def lanes(k):
         return pl.ds(k * CHUNK, CHUNK)
 
@@ -84,6 +99,8 @@
 
     for kind in range(2):
         total[kind, :, packed - 128:] = jnp.zeros((HD, 128), F32)
+    for one in small:
+        one.wait()
     frames = embed_ref.shape[0]
     ids = lax.broadcasted_iota(jnp.int32, (frames, 2 * CL), 0)
     block = lax.broadcasted_iota(jnp.int32, (frames, 2 * CL), 1) < CL
@@ -93,6 +110,8 @@
     def act_until(end):
         while acted[0] < end:
             part = slice(acted[0], min(acted[0] + CHUNK, width))
+            for which in range(4):
+                load(acted[0] // CHUNK, which).wait()
             shift = dot(embed_ref[:, part], onehot, ((0,), (0,)))
             act[part] = jnp.maximum(k_ref[part].astype(F32) + shift, 0.0).astype(BF16)
             acted[0] = part.stop
@@ -184,21 +203,35 @@
 
     written = [0]
 
+    def store(which, start, stop, k):
+        src, dst = ((out_ref, out_hbm), (qg_ref, qg_hbm), (kg_ref, kg_hbm), (vg_ref, vg_hbm))[which]
+        part = pl.ds(start * HD, (stop - start) * HD)
+        return pltpu.make_async_copy(src.at[part], dst.at[part], store_sem.at[which, k])
+
+    stores = []
+
     def stage_e(k):
         sib_last(k).wait_recv()
+        begin = written[0]
         while written[0] < HEADS and (written[0] + 1) * HD <= (k + 1) * CHUNK:
             head_out(written[0])
             written[0] += 1
+        for which in range(4):
+            stores.append(store(which, begin, written[0], k))
+            stores[-1].start()
 
     order = []
     for k in range(chunks + 1):
         order += [(stage_a, k), (stage_b, k - 1)]
-    for k in range(chunks + 4):
-        order += [(stage_c, k), (stage_d, k - 2), (stage_e, k - 4)]
+    order += [(stage_c, k) for k in range(chunks)]
+    for k in range(chunks + 1):
+        order += [(stage_d, k), (stage_e, k - 1)]
     for stage, k in order:
         if 0 <= k < chunks:
             stage(k)
 
+    for one in stores:
+        one.wait()
     for k in range(chunks):
         sib_first(k).wait_send()
         pair_first(k).wait_send()
@@ -211,19 +244,50 @@
             chain(k).wait_send()
 
 
+def finish(*refs):
+    srcs, dsts, holds, (in_sem, out_sem) = refs[:4], refs[4:8], refs[8:12], refs[12:]
+    size = srcs[0].shape[0] // PIECES
+    loads, stores = [], []
+    for i in range(4):
+        for p in range(PIECES):
+            part = pl.ds(p * size, size)
+            loads.append(pltpu.make_async_copy(srcs[i].at[part], holds[i].at[part], in_sem.at[i, p]))
+            stores.append(pltpu.make_async_copy(holds[i].at[part], dsts[i].at[part], out_sem.at[i, p]))
+    for one in loads:
+        one.start()
+    for load, store in zip(loads, stores):
+        load.wait()
+        store.start()
+    for one in stores:
+        one.wait()
+
+
 def local(query_pre, key_pre, values, out_grad, block_frame, frame_embed):
     n = lax.axis_size("group")
     rows, width = query_pre.shape
     packed = -(-width // CHUNK) * CHUNK
     chunks = packed // CHUNK
-    vmem = pl.BlockSpec(memory_space=pltpu.VMEM)
+    hbm = pl.BlockSpec(memory_space=pltpu.HBM)
     result = jax.ShapeDtypeStruct((width, rows), BF16)
     outs = pl.pallas_call(
         functools.partial(kernel, n, width),
         out_shape=(result,) * 4,
-        in_specs=[vmem] * 4 + [pl.BlockSpec(memory_space=pltpu.SMEM), vmem],
-        out_specs=(vmem,) * 4,
+        in_specs=[hbm] * 6,
+        out_specs=(hbm,) * 4,
         scratch_shapes=[
+            pltpu.VMEM((width, rows), BF16),
+            pltpu.VMEM((width, rows), BF16),
+            pltpu.VMEM((width, rows), BF16),
+            pltpu.VMEM((width, rows), BF16),
+            pltpu.SemaphoreType.DMA((4, chunks)),
+            pltpu.VMEM((width, rows), BF16),
+            pltpu.VMEM((width, rows), BF16),
+            pltpu.VMEM((width, rows), BF16),
+            pltpu.VMEM((width, rows), BF16),
+            pltpu.SMEM(block_frame.shape, jnp.int32),
+            pltpu.VMEM(frame_embed.shape, BF16),
+            pltpu.SemaphoreType.DMA((4, chunks)),
+            pltpu.SemaphoreType.DMA((2,)),
             pltpu.VMEM((width, rows), BF16),
             pltpu.VMEM((2, HD, packed), F32),
             pltpu.VMEM((2, HEADS, HD, HD), F32),
@@ -240,8 +304,15 @@
             pltpu.SemaphoreType.DMA((5, chunks)),
         ],
         compiler_params=pltpu.CompilerParams(
-            collective_id=0, has_side_effects=True, vmem_limit_bytes=44 * 1024 * 1024),
+            collective_id=0, has_side_effects=True, vmem_limit_bytes=63 * 1024 * 1024),
     )(query_pre.T, key_pre.T, values.T, out_grad.T, block_frame, frame_embed)
+    outs = pl.pallas_call(
+        finish,
+        out_shape=(result,) * 4,
+        in_specs=[hbm] * 4,
+        out_specs=(hbm,) * 4,
+        scratch_shapes=[pltpu.VMEM((width, rows), BF16)] * 4 + [pltpu.SemaphoreType.DMA((4, PIECES))] * 2,
+    )(*outs)
     return tuple(out.T for out in outs)
 
 

time: 50.8 us -> 41.1 us (0.81)
  local copies, waits for them, and re-layouts: 9.02 us -> 0 us
  Pallas kernels: 40.8 us -> 39.8 us
    unnamed x16 -> x0, local copies, waits for them, and re-layouts: 9.02 us -> none
    pallas_call x1, Pallas kernels: 40.8 us -> 37.3 us  [local(): pl.pallas_call(functools.partial(kernel, n, width), out_shape=(result,) *...]
    pallas_call x0 -> x1, Pallas kernels: none -> 2.47 us  [local(): pl.pallas_call(finish, out_shape=(result,) * 4, in_specs=[hbm] * 4, out_s...]
where the time goes in v3:
time: 41.1 us; the launch traced here: 40.4 us
  Pallas kernels  39.8 us (97%)
  between operations  0.64 us (2%)
    pallas_call x1, Pallas kernels, local(): pl.pallas_call(functools.partial(kernel, n, width), out_shape=(result,) *...  37.3 us
    pallas_call x1, Pallas kernels, local(): pl.pallas_call(finish, out_shape=(result,) * 4, in_specs=[hbm] * 4, out_s...  2.47 us

profile of v3, /device:TPU:1, one launch (start us, length us, event | category | flops | bytes accessed | tf_op | source)
XLA Modules:
  0.0 40.4 jit_solution(16026337066738479905)
XLA Ops:
  0.6 37.3 %shard_map.93 = (bf16[2240,128]{1,0:T(8,128)(2,1)}, bf16[2240,128]{1,0:T(8,128)(2,1)}, bf16[2240,128]{1,0:T(8,128)(2,1)}, bf16[2240,128]{1,0:T(8,128)(2,1)}) custom-call(bf16[2240,128]{1,0:T(8,128)(2,1)} %bitcast.8, bf16[2240,128]{1,0:T(8,128)(2,1)} %bitcast.9, bf16[2240,128]{1,0:T(8,128)(2,1)} %bitcast.10, bf16[2240,128]{1,0:T(8,128)(2,1)} %bitcast.11, ...), custom_call_target="tpu_custom_call" | custom-call | tf_op jit(solution)/shard_map/pallas_call | solution.py:272
  38.0 2.5 %shard_map.94 = (bf16[2240,128]{1,0:T(8,128)(2,1)}, bf16[2240,128]{1,0:T(8,128)(2,1)}, bf16[2240,128]{1,0:T(8,128)(2,1)}, bf16[2240,128]{1,0:T(8,128)(2,1)}) custom-call(bf16[2240,128]{1,0:T(8,128)(2,1)} %get-tuple-element.12.refs_0_, bf16[2240,128]{1,0:T(8,128)(2,1)} %get-tuple-element.13.refs_1_, bf16[2240,128]{1,0:T(8,128)(2,1)} %get-tuple-element.14.refs_2_, ...), custom_call_target="tpu_custom_call" | custom-call | tf_op jit(solution)/shard_map/pallas_call | solution.py:309

commit v4 on v3

--- a/solution.py
+++ b/solution.py
@@ -221,8 +221,8 @@
             stores[-1].start()
 
     order = []
-    for k in range(chunks + 1):
-        order += [(stage_a, k), (stage_b, k - 1)]
+    for k in range(chunks + 2):
+        order += [(stage_a, k), (stage_b, k - 2)]
     order += [(stage_c, k) for k in range(chunks)]
     for k in range(chunks + 1):
         order += [(stage_d, k), (stage_e, k - 1)]

time: 41.1 us -> 40.7 us (level)
  no operation moved by 1% of the time
where the time goes in v4:
time: 40.7 us; the launch traced here: 40.1 us
  Pallas kernels  39.4 us (97%)
  between operations  0.64 us (2%)
    pallas_call x1, Pallas kernels, local(): pl.pallas_call(functools.partial(kernel, n, width), out_shape=(result,) *...  36.9 us
    pallas_call x1, Pallas kernels, local(): pl.pallas_call(finish, out_shape=(result,) * 4, in_specs=[hbm] * 4, out_s...  2.47 us

profile of v4, /device:TPU:1, one launch (start us, length us, event | category | flops | bytes accessed | tf_op | source)
XLA Modules:
  0.0 40.1 jit_solution(4225794763317301650)
XLA Ops:
  0.6 36.9 %shard_map.93 = (bf16[2240,128]{1,0:T(8,128)(2,1)}, bf16[2240,128]{1,0:T(8,128)(2,1)}, bf16[2240,128]{1,0:T(8,128)(2,1)}, bf16[2240,128]{1,0:T(8,128)(2,1)}) custom-call(bf16[2240,128]{1,0:T(8,128)(2,1)} %bitcast.8, bf16[2240,128]{1,0:T(8,128)(2,1)} %bitcast.9, bf16[2240,128]{1,0:T(8,128)(2,1)} %bitcast.10, bf16[2240,128]{1,0:T(8,128)(2,1)} %bitcast.11, ...), custom_call_target="tpu_custom_call" | custom-call | tf_op jit(solution)/shard_map/pallas_call | solution.py:272
  37.6 2.5 %shard_map.94 = (bf16[2240,128]{1,0:T(8,128)(2,1)}, bf16[2240,128]{1,0:T(8,128)(2,1)}, bf16[2240,128]{1,0:T(8,128)(2,1)}, bf16[2240,128]{1,0:T(8,128)(2,1)}) custom-call(bf16[2240,128]{1,0:T(8,128)(2,1)} %get-tuple-element.12.refs_0_, bf16[2240,128]{1,0:T(8,128)(2,1)} %get-tuple-element.13.refs_1_, bf16[2240,128]{1,0:T(8,128)(2,1)} %get-tuple-element.14.refs_2_, ...), custom_call_target="tpu_custom_call" | custom-call | tf_op jit(solution)/shard_map/pallas_call | solution.py:309
